TPU v7x, 128 devices: a whole 4x4x4 slice. The times are simulated.
128 devices in a mesh: pipe: 2 (over y_hi), seq: 16 (over x, z), dp: 4 (over y_lo, core).
Axes of the slice: x: 4, y: 4 (y_hi: 2, y_lo: 2; y = y_hi * 2 + y_lo), z: 4, core: 2. Of those that a mesh axis runs over, the one named last changes fastest.
Arguments:
- queries: bfloat16 [2, 4, 16, 384, 1536], P('pipe', 'dp', 'seq'), may hold values from -18 to 18
- keys: bfloat16 [2, 4, 16, 384, 1536], P('pipe', 'dp', 'seq'), may hold values from -18 to 18
- values: bfloat16 [2, 4, 16, 384, 1536], P('pipe', 'dp', 'seq'), may hold values from -6 to 6
- grad_out: bfloat16 [2, 4, 16, 384, 1536], P('pipe', 'dp', 'seq'), may hold values from -20 to 20
- norm_gains: float32 [2, 2, 128], P('pipe'), may hold values from 0.5 to 1.5
- kv_tiles: int32 [2, 4, 16, 3], P('pipe', 'dp', 'seq'), may hold values from -1 to 15, as said below
Outputs:
- qkv_grad: bfloat16 [2, 3, 4, 16, 384, 1536], P('pipe', None, 'dp', 'seq')
- gain_grads: float32 [2, 2, 128], P('pipe')
Inputs may be any that keep to these rules, and one draw needn't show every extreme that they name: `kv_tiles`: tile t covers frame tile t // 1 and spatial tile t % 1. The row of tile t names tile t itself and some of the other tiles of frame tiles t - 1, t // 1 and t + 1 inside the sample, each at most once, in some order; its other entries are -1.
All inputs are finite; a program needn't handle non-finite values.
Results may differ from a plain program's by a relative error of at most 0.007.
Values may be sent and summed in bfloat16 or wider, within the bound.
A program may use at most 256 MiB of HBM per device.

v0:
```python
import math
import jax
import jax.numpy as jnp
from jax import lax
from jax.sharding import PartitionSpec as P

HEADS = 12
HEAD_DIM = 128
epsilon = 1e-06


def padded(shard, sides, width):
    for axis, dim in sides:
        size, length = (lax.axis_size(axis), shard.shape[dim])
        up = [(i, (i + 1) % size) for i in range(size - 1)]
        down = [(j, i) for i, j in up]
        last = lax.slice_in_dim(shard, length - width, length, axis=dim)
        initial = lax.slice_in_dim(shard, 0, width, axis=dim)
        before = lax.ppermute(last, axis, up)
        after = lax.ppermute(initial, axis, down)
        shard = jnp.concatenate([before, shard, after], axis=dim)
    return shard


def passed_along(value, axis, steps):
    count = lax.axis_size(axis)
    initial, last = (max(0, -steps), min(count, count - steps))
    return lax.ppermute(value, axis, [(source, source + steps) for source in range(initial, last)])


def passed_along_2(value, axis, steps):
    count = lax.axis_size(axis)
    pairs = [(source, (source + steps) % count) for source in range(count)]
    return lax.ppermute(value, axis, pairs)


def normalize(source, gain_row):
    floats = source.astype(jnp.float32).reshape(source.shape[:-1] + (HEADS, HEAD_DIM))
    scaled = lax.rsqrt(jnp.mean(floats * floats, axis=-1, keepdims=True) + epsilon)
    normed = (floats * scaled * gain_row).astype(jnp.bfloat16).reshape(source.shape)
    return (normed, floats, scaled)


def norm_back(grad_hat, floats, scaled, gain_row):
    projected = jnp.sum(gain_row * grad_hat * floats, axis=-1, keepdims=True)
    gradient = scaled * gain_row * grad_hat - scaled**3 * floats * projected / HEAD_DIM
    gain_part = jnp.sum((grad_hat * floats * scaled).reshape(-1, HEAD_DIM), axis=0)
    return (gradient.reshape(gradient.shape[:-2] + (HEADS * HEAD_DIM,)), gain_part)


def score_block(query_head, grad_head, key_head, value_head, key_mask):
    root_scale = HEAD_DIM ** (-0.5)
    scores = (
        jnp.einsum("nqhd,nkhd->nhqk", query_head, key_head, preferred_element_type=jnp.float32)
        * root_scale
    )
    exp_scores = jnp.exp(scores) * key_mask[:, None, None, :]
    grad_attn = jnp.einsum(
        "nqhd,nkhd->nhqk", grad_head, value_head, preferred_element_type=jnp.float32
    )
    totals = jnp.sum(exp_scores, axis=-1, keepdims=True)
    attention = exp_scores / totals
    deltas = jnp.sum(attention * grad_attn, axis=-1, keepdims=True)
    dscore = (attention * (grad_attn - deltas)).astype(jnp.bfloat16)
    return (dscore, attention.astype(jnp.bfloat16), totals, deltas)


def spread(slot_grad, targets, list_slots, target_span):
    row_count, key_rows, head_count, head_width = slot_grad.shape
    shaped = slot_grad.reshape(
        row_count * list_slots, key_rows // list_slots, head_count * head_width
    )
    flat_targets = targets.reshape(-1)
    placed = jnp.where(flat_targets >= 0, flat_targets, target_span)
    totals = jnp.zeros(
        (target_span + 1, key_rows // list_slots, head_count * head_width), jnp.float32
    )
    return totals.at[placed].add(shaped)[:target_span]


def tile_pass(
    query_hat, grad_in, key_gathered, value_gathered, key_mask, targets, list_slots, target_span
):
    row_count, tile_rows, lane_total = query_hat.shape
    key_rows = key_gathered.shape[1]
    root_scale = HEAD_DIM ** (-0.5)
    query_parts, key_parts, value_parts, total_parts, delta_parts = ([], [], [], [], [])
    for first_head in range(0, HEADS, 2):
        lane_span = slice(first_head * HEAD_DIM, (first_head + 2) * HEAD_DIM)
        query_head = query_hat[:, :, lane_span].reshape(row_count, tile_rows, 2, HEAD_DIM)
        grad_head = grad_in[:, :, lane_span].reshape(row_count, tile_rows, 2, HEAD_DIM)
        key_head = key_gathered[:, :, lane_span].reshape(row_count, key_rows, 2, HEAD_DIM)
        value_head = value_gathered[:, :, lane_span].reshape(row_count, key_rows, 2, HEAD_DIM)
        dscore, attn_low, totals, deltas = score_block(
            query_head, grad_head, key_head, value_head, key_mask
        )
        query_parts.append(
            jnp.einsum("nhqk,nkhd->nqhd", dscore, key_head, preferred_element_type=jnp.float32)
            * root_scale
        )
        key_slot = (
            jnp.einsum("nhqk,nqhd->nkhd", dscore, query_head, preferred_element_type=jnp.float32)
            * root_scale
        )
        value_slot = jnp.einsum(
            "nhqk,nqhd->nkhd", attn_low, grad_head, preferred_element_type=jnp.float32
        )
        key_parts.append(spread(key_slot, targets, list_slots, target_span))
        value_parts.append(spread(value_slot, targets, list_slots, target_span))
        total_parts.append(totals[..., 0])
        delta_parts.append(deltas[..., 0])
    query_grads = jnp.concatenate(query_parts, axis=2)
    return (
        query_grads,
        jnp.concatenate(key_parts, axis=-1),
        jnp.concatenate(value_parts, axis=-1),
        jnp.concatenate(total_parts, axis=1),
        jnp.concatenate(delta_parts, axis=1),
    )


def local(queries, keys, values, grad_out, norm_gains, kv_tiles):
    query_in = queries[0, 0]
    key_in = keys[0, 0]
    value_in = values[0, 0]
    grad_in = grad_out[0, 0]
    gain_rows = norm_gains[0]
    tile_lists = kv_tiles[0, 0]
    tiles_here, tile_rows, lane_total = query_in.shape
    list_slots = tile_lists.shape[1]
    position = lax.axis_index("seq")
    seq_count = lax.axis_size("seq")
    query_hat, query_floats, query_scale = normalize(query_in, gain_rows[0])
    key_hat, key_floats, key_scale = normalize(key_in, gain_rows[1])
    rim_pairs = padded(jnp.stack([key_hat, value_in]), (("seq", 1),), tiles_here)
    live_slots = tile_lists >= 0
    key_mask = jnp.repeat(live_slots.astype(jnp.float32), tile_rows, axis=1)
    local_ids = tile_lists - (position - 1) * tiles_here
    fetch_ids = jnp.clip(local_ids, 0, 3 * tiles_here - 1)
    key_gathered = rim_pairs[0][fetch_ids].reshape(tiles_here, list_slots * tile_rows, lane_total)
    value_gathered = rim_pairs[1][fetch_ids].reshape(tiles_here, list_slots * tile_rows, lane_total)
    targets = jnp.where(live_slots, local_ids, -1)
    target_span = 3 * tiles_here
    query_hat_grad, key_acc, value_acc, totals, deltas = tile_pass(
        query_hat, grad_in, key_gathered, value_gathered, key_mask, targets, list_slots, target_span
    )
    query_grad, query_gain = norm_back(query_hat_grad, query_floats, query_scale, gain_rows[0])
    query_low = query_grad.astype(jnp.bfloat16)
    from_right = passed_along(jnp.stack([key_acc[:tiles_here], value_acc[:tiles_here]]), "seq", -1)
    from_left = passed_along(
        jnp.stack([key_acc[2 * tiles_here :], value_acc[2 * tiles_here :]]), "seq", 1
    )
    key_hat_grad = key_acc[tiles_here : 2 * tiles_here] + from_right[0] + from_left[0]
    value_grad = value_acc[tiles_here : 2 * tiles_here] + from_right[1] + from_left[1]
    key_grad, key_gain = norm_back(
        key_hat_grad.reshape(tiles_here, tile_rows, HEADS, HEAD_DIM),
        key_floats,
        key_scale,
        gain_rows[1],
    )
    summed = lax.psum(jnp.stack([query_gain, key_gain]), ("seq", "dp"))
    gain_grads = summed / math.sqrt(
        lax.axis_size("dp") * seq_count * tiles_here * tile_rows * HEADS
    )
    key_low = key_grad.astype(jnp.bfloat16)
    value_low = value_grad.astype(jnp.bfloat16)
    passed = passed_along_2(jnp.stack([query_low, key_low, value_low]), "pipe", -1)
    return (passed[None, :, None], gain_grads[None])


def solution(mesh):
    placed = (
        P("pipe", "dp", "seq", None, None),
        P("pipe", "dp", "seq", None, None),
        P("pipe", "dp", "seq", None, None),
        P("pipe", "dp", "seq", None, None),
        P("pipe", None, None),
        P("pipe", "dp", "seq", None),
    )
    return jax.shard_map(
        local,
        mesh=mesh,
        in_specs=placed,
        out_specs=(P("pipe", None, "dp", "seq", None, None), P("pipe", None, None)),
        check_vma=False,
    )
```

profile of v0, /device:TPU:16, one launch (start us, length us, event | category | flops | bytes accessed | tf_op | source)
XLA Modules:
  0.0 747.3 jit_solution(4585193369530839053)
XLA Ops:
  10.4 5.3 collective-permute-start
  40.4 24.8 %collective-permute-done = bf16[2,1,384,1536]{3,2,1,0:T(8,128)(2,1)} collective-permute-done((bf16[2,1,384,1536]{3,2,1,0:T(8,128)(2,1)}, bf16[2,1,384,1536]{3,2,1,0:T(8,128)(2,1)}, u32[]{:S(2)}, u32[]{:S(2)}) %collective-permute-start) | collective-permute-done | bytes 2359328 | tf_op jit(solution)/shard_map/ppermute | solution.py:19
  65.2 5.5 collective-permute-done.1
  70.7 3.9 pad_maximum_fusion
  74.6 3.8 slice_bitcast_fusion
  78.4 4.7 gather_fusion.1
  83.1 3.5 fusion.83
  87.6 4.7 gather_fusion
  92.3 3.6 fusion.84
  98.0 3.6 convolution_bitcast_fusion.5
  101.6 5.2 multiply_reduce_fusion.5
  106.8 4.0 convolution_bitcast_fusion.11
  110.8 3.6 multiply_convert_fusion.5
  118.7 3.6 convolution_bitcast_fusion.4
  122.2 5.2 multiply_reduce_fusion.4
  127.5 4.0 convolution_bitcast_fusion.10
  131.5 3.7 multiply_convert_fusion.4
  139.4 3.6 convolution_bitcast_fusion.3
  143.0 5.2 multiply_reduce_fusion.3
  148.2 4.0 convolution_bitcast_fusion.9
  152.2 3.8 multiply_convert_fusion.3
  160.3 3.6 convolution_bitcast_fusion.2
  163.8 5.2 multiply_reduce_fusion.2
  169.1 4.0 convolution_bitcast_fusion.8
  173.0 3.7 multiply_convert_fusion.2
  181.0 3.6 convolution_bitcast_fusion.1
  184.6 5.2 multiply_reduce_fusion.1
  189.8 4.0 convolution_bitcast_fusion.7
  193.8 3.7 multiply_convert_fusion.1
  198.8 3.8 convolution_bitcast_fusion
  202.6 5.0 multiply_reduce_fusion
  207.7 4.0 convolution_bitcast_fusion.6
  211.6 3.7 multiply_convert_fusion
  217.8 3.3 reshape.1253
  228.6 3.2 scatter_fusion
  262.7 3.3 scatter_fusion.1
  269.8 3.3 scatter_fusion.2
  276.8 3.3 scatter_fusion.3
  283.9 3.3 scatter_fusion.4
  291.0 3.6 scatter_fusion.5
  297.0 5.0 slice_bitcast_fusion.9
  302.0 4.3 copy.292
  308.3 4.7 copy.289
  316.7 3.2 scatter_fusion.6
  322.5 4.3 copy.295
  328.8 4.9 copy.298
  335.7 4.7 copy.301
  342.4 4.7 copy.304
  350.9 3.2 scatter_fusion.7
  357.9 3.2 scatter_fusion.8
  365.0 3.2 scatter_fusion.9
  372.1 3.2 scatter_fusion.10
  379.2 3.5 scatter_fusion.11
  394.5 6.7 collective-permute-start.3
  404.8 3.3 copy.278
  420.8 74.6 %collective-permute-done.2 = f32[2,1,384,1536]{3,2,1,0:T(8,128)} collective-permute-done((f32[2,1,384,1536]{3,2,1,0:T(8,128)}, f32[2,1,384,1536]{3,2,1,0:T(8,128)}, u32[]{:S(2)}, u32[]{:S(2)}) %collective-permute-start.2) | collective-permute-done | bytes 4718624 | tf_op jit(solution)/shard_map/ppermute | solution.py:28
  495.4 3.7 collective-permute-done.3
  499.0 7.3 fusion.21
  508.3 4.9 multiply_reduce_fusion.8
  522.7 4.5 fusion.65
  541.6 3.2 copy.308
  549.2 3.6 multiply_reduce_fusion.6
  552.9 189.6 %psum.7 = f32[2,128]{1,0:T(2,128)S(1)} all-reduce(f32[2,128]{1,0:T(2,128)S(1)} %pad_maximum_fusion.5), channel_id=1, replica_groups=mesh['pipe'=2,'seq'=16,'dp'=4] {'seq','dp'}, use_global_device_ids=true, to_apply=%region_31.32 | all-reduce | flops 256 | bytes 2048 | tf_op jit(solution)/shard_map/psum | solution.py:161
  743.0 4.0 copy.394
  (273 shorter events, 206.3 us)
Async XLA Ops:
  2.2 2.6 copy-start.2
  4.8 2.2 copy-start.72
  4.8 2.7 copy-start.5
  7.0 15.9 %copy-start.70 = (f32[128]{0:T(128)}, f32[128]{0:T(128)S(1)}, u32[]{:S(2)}) copy-start(f32[128]{0:T(128)S(1)} %get-tuple-element.45) | copy-start | bytes 1540
  8.1 2.3 copy-start.23
  8.8 8.3 %copy-start.55 = (bf16[1,1,1,384,1536]{4,3,2,1,0:T(8,128)(2,1)S(1)}, bf16[1,1,1,384,1536]{4,3,2,1,0:T(8,128)(2,1)}, u32[]{:S(2)}) copy-start(bf16[1,1,1,384,1536]{4,3,2,1,0:T(8,128)(2,1)} %param.9) | copy-start | bytes 3538948
  10.4 8.1 %copy-start.7 = (bf16[1,1,1,384,1536]{4,3,2,1,0:T(8,128)(2,1)S(1)}, bf16[1,1,1,384,1536]{4,3,2,1,0:T(8,128)(2,1)}, u32[]{:S(2)}) copy-start(bf16[1,1,1,384,1536]{4,3,2,1,0:T(8,128)(2,1)} %param.6) | copy-start | bytes 3538948
  10.4 54.8 %collective-permute-start = (bf16[2,1,384,1536]{3,2,1,0:T(8,128)(2,1)}, bf16[2,1,384,1536]{3,2,1,0:T(8,128)(2,1)}, u32[]{:S(2)}, u32[]{:S(2)}) collective-permute-start(bf16[2,1,384,1536]{3,2,1,0:T(8,128)(2,1)} %pad_maximum_fusion.4), channel_id=1, source_target_pairs={{0,4},{4,8},{8,12},{12,16},{16,20},{20,24},{24,28},{28,32},{32,36}... | collective-permute-start | bytes 7077896 | tf_op jit(solution)/shard_map/ppermute | solution.py:19
  15.8 54.9 %collective-permute-start.1 = (bf16[2,1,384,1536]{3,2,1,0:T(8,128)(2,1)}, bf16[2,1,384,1536]{3,2,1,0:T(8,128)(2,1)}, u32[]{:S(2)}, u32[]{:S(2)}) collective-permute-start(bf16[2,1,384,1536]{3,2,1,0:T(8,128)(2,1)} %pad_maximum_fusion.4), channel_id=1, source_target_pairs={{4,0},{8,4},{12,8},{16,12},{20,16},{24,20},{28,24},{32,28},{36,32}... | collective-permute-start | bytes 7077896 | tf_op jit(solution)/shard_map/ppermute | solution.py:20
  20.7 380.5 %copy-start = (f32[384,12,128]{0,2,1:T(8,128)}, f32[384,12,128]{0,2,1:T(8,128)S(1)}, u32[]{:S(2)}) copy-start(f32[384,12,128]{0,2,1:T(8,128)S(1)} %mul.607) | copy-start | bytes 7077892
  22.9 2.0 copy-start.66
  24.9 2.9 copy-start.73
  26.0 44.7 %copy-start.24 = (bf16[1,1,384,1536]{3,2,1,0:T(8,128)(2,1)S(1)}, bf16[1,1,384,1536]{3,2,1,0:T(8,128)(2,1)}, u32[]{:S(2)}) copy-start(bf16[1,1,384,1536]{3,2,1,0:T(8,128)(2,1)} %copy-done.23) | copy-start | bytes 3538948
  36.6 34.1 %copy-start.33 = (bf16[1,1,1,384,1536]{4,3,2,1,0:T(8,128)(2,1)S(1)}, bf16[1,1,1,384,1536]{4,3,2,1,0:T(8,128)(2,1)}, u32[]{:S(2)}) copy-start(bf16[1,1,1,384,1536]{4,3,2,1,0:T(8,128)(2,1)} %param.8) | copy-start | bytes 3538948
  106.8 4.0 copy-start.18
  127.5 4.0 copy-start.19
  148.2 4.0 copy-start.20
  169.1 4.0 copy-start.21
  189.8 4.0 copy-start.22
  198.8 8.9 %copy-start.52 = (bf16[1,1152,256]{1,2,0:T(8,128)(2,1)}, bf16[1,1152,256]{1,2,0:T(8,128)(2,1)S(1)}, u32[]{:S(2)}) copy-start(bf16[1,1152,256]{1,2,0:T(8,128)(2,1)S(1)} %copy.364) | copy-start | bytes 1769476
  198.8 3.8 copy-start.56
  202.6 5.0 copy-start.54
  207.7 4.0 copy-start.17
  211.6 3.7 copy-start.10
  211.6 3.7 copy-start.58
  231.8 2.6 copy-start.12
  231.9 2.6 copy-start.57
  258.2 4.5 copy-start.36
  265.9 3.9 copy-start.42
  273.1 3.8 copy-start.40
  280.1 3.8 copy-start.39
  287.2 3.8 copy-start.38
  297.0 5.0 copy-start.34
  320.0 2.6 copy-start.35
  354.1 3.8 copy-start.45
  361.2 3.9 copy-start.44
  368.3 3.8 copy-start.43
  375.3 3.9 copy-start.37
  385.1 3.1 copy-start.30
  388.2 3.9 copy-start.29
  390.8 104.6 %collective-permute-start.2 = (f32[2,1,384,1536]{3,2,1,0:T(8,128)}, f32[2,1,384,1536]{3,2,1,0:T(8,128)}, u32[]{:S(2)}, u32[]{:S(2)}) collective-permute-start(f32[2,1,384,1536]{3,2,1,0:T(8,128)} %pad_maximum_fusion.1), channel_id=1, source_target_pairs={{4,0},{8,4},{12,8},{16,12},{20,16},{24,20},{28,24},{32,28},{36,32}... | collective-permute-start | bytes 14155784 | tf_op jit(solution)/shard_map/ppermute | solution.py:28
  394.5 104.5 %collective-permute-start.3 = (f32[2,1,384,1536]{3,2,1,0:T(8,128)}, f32[2,1,384,1536]{3,2,1,0:T(8,128)}, u32[]{:S(2)}, u32[]{:S(2)}) collective-permute-start(f32[2,1,384,1536]{3,2,1,0:T(8,128)} %pad_maximum_fusion.2), channel_id=1, source_target_pairs={{0,4},{4,8},{8,12},{12,16},{16,20},{20,24},{24,28},{28,32},{32,36}... | collective-permute-start | bytes 14155784 | tf_op jit(solution)/shard_map/ppermute | solution.py:28
  401.2 2.0 copy-start.62
  404.8 3.3 copy-start.4
  408.1 2.0 copy-start.61
  410.2 2.0 copy-start.47
  410.2 4.3 copy-start.48
  412.2 2.3 copy-start.11
  412.2 3.0 copy-start.13
  412.2 3.0 copy-start.49
  418.6 2.1 copy-start.1
  506.3 2.0 copy-start.69
  506.4 2.0 copy-start.71
  519.4 3.2 copy-start.6
  519.4 3.2 copy-start.65
  522.6 4.6 copy-start.8
  522.6 4.6 copy-start.25
  522.6 4.8 copy-start.26
  522.6 5.5 copy-start.27
  522.6 6.2 copy-start.28
  522.7 6.2 copy-start.67
  532.1 210.9 %collective-permute-start.4 = (bf16[3,1,384,1536]{3,2,1,0:T(8,128)(2,1)}, bf16[3,1,384,1536]{3,2,1,0:T(8,128)(2,1)}, u32[]{:S(2)}, u32[]{:S(2)}) collective-permute-start(bf16[3,1,384,1536]{3,2,1,0:T(8,128)(2,1)} %pad_maximum_fusion.3), channel_id=1, source_target_pairs={{0,64},{64,0},{1,65},{65,1},{2,66},{66,2},{3,67},{67,3},{4,68},{68... | collective-permute-start | bytes 10616840 | tf_op jit(solution)/shard_map/ppermute | solution.py:34
  537.7 3.1 copy-start.59
  541.6 3.2 copy-start.9
  (15 other events, 21.8 us)
where the time goes:
time: 754 us; the launch traced here: 747 us
  local copies, waits for them, and re-layouts  235 us (31%)
  blocking collectives  190 us (25%)
  waiting for transfers between devices  109 us (14%)
  other arithmetic  105 us (14%)
  matrix products  91.6 us (12%)
  starting transfers between devices  16.1 us (2%)
    psum x1, blocking collectives, local(): summed = lax.psum(jnp.stack([query_gain, key_gain]), ('seq', 'dp'))  190 us
    ppermute x2, waiting for transfers between devices, passed_along(): lax.ppermute(value, axis, [(source, source + steps) for source in range(i...  78.3 us
    unnamed x172, local copies, waits for them, and re-layouts  58.3 us
    scatter-add x12, other arithmetic, spread(): return totals.at[placed].add(shaped)[:target_span]  39.6 us
    div x6, matrix products, score_block(): attention = exp_scores / totals  31.2 us
    reshape x12, local copies, waits for them, and re-layouts, spread(): slot_grad.reshape(row_count * list_slots, key_rows // list_slots, head_co...  29.8 us
    transpose x6, local copies, waits for them, and re-layouts, tile_pass(): jnp.einsum('nhqk,nqhd->nkhd', attn_low, grad_head, preferred_element_type...  27.7 us
    ppermute x1, waiting for transfers between devices, padded(): before = lax.ppermute(last, axis, up)  24.8 us
  transfers between devices with their start and end apart: 5, of which 4 were waited for; matrix products, arithmetic and copies ran while one was open for 9% of the time, Pallas kernels for 0%

commit v1 on v0

--- a/solution.py
+++ b/solution.py
@@ -158,7 +158,7 @@
         key_scale,
         gain_rows[1],
     )
-    summed = lax.psum(jnp.stack([query_gain, key_gain]), ("seq", "dp"))
+    summed = lax.psum(lax.psum(jnp.stack([query_gain, key_gain]), axis_name="dp"), axis_name="seq")
     gain_grads = summed / math.sqrt(
         lax.axis_size("dp") * seq_count * tiles_here * tile_rows * HEADS
     )

time: 754 us -> 669 us (0.89)
  blocking collectives: 190 us -> 102 us
    psum x1 -> x2, blocking collectives: 190 us -> 102 us  [the longest x1 59.3 us: local(): lax.psum(jnp.stack([query_gain, key_gain]), axis_name='dp')]
  transfers between devices with their start and end apart: 5 -> 5, of which waited for: 4 -> 4; matrix products, arithmetic and copies ran while one was open for 9% -> 10% of each run, Pallas kernels for 0% -> 0%
where the time goes in v1:
time: 669 us; the launch traced here: 659 us
  local copies, waits for them, and re-layouts  235 us (35%)
  waiting for transfers between devices  108 us (16%)
  other arithmetic  105 us (16%)
  blocking collectives  102 us (15%)
  matrix products  91.6 us (14%)
  starting transfers between devices  16.1 us (2%)
    ppermute x2, waiting for transfers between devices, passed_along(): lax.ppermute(value, axis, [(source, source + steps) for source in range(i...  78.1 us
    psum x1, blocking collectives, local(): lax.psum(jnp.stack([query_gain, key_gain]), axis_name='dp')  59.3 us
    unnamed x172, local copies, waits for them, and re-layouts  58.2 us
    psum x1, blocking collectives, local(): lax.psum(lax.psum(jnp.stack([query_gain, key_gain]), axis_name='dp'), axi...  42.3 us
    scatter-add x12, other arithmetic, spread(): return totals.at[placed].add(shaped)[:target_span]  39.6 us
    div x6, matrix products, score_block(): attention = exp_scores / totals  31.3 us
    reshape x12, local copies, waits for them, and re-layouts, spread(): slot_grad.reshape(row_count * list_slots, key_rows // list_slots, head_co...  29.8 us
    transpose x6, local copies, waits for them, and re-layouts, tile_pass(): jnp.einsum('nhqk,nqhd->nkhd', attn_low, grad_head, preferred_element_type...  27.7 us
  transfers between devices with their start and end apart: 5, of which 4 were waited for; matrix products, arithmetic and copies ran while one was open for 10% of the time, Pallas kernels for 0%

profile of v1, /device:TPU:16, one launch (start us, length us, event | category | flops | bytes accessed | tf_op | source)
XLA Modules:
  0.0 659.4 jit_solution(4529768686161955279)
XLA Ops:
  10.4 5.3 collective-permute-start
  40.4 24.8 %collective-permute-done = bf16[2,1,384,1536]{3,2,1,0:T(8,128)(2,1)} collective-permute-done((bf16[2,1,384,1536]{3,2,1,0:T(8,128)(2,1)}, bf16[2,1,384,1536]{3,2,1,0:T(8,128)(2,1)}, u32[]{:S(2)}, u32[]{:S(2)}) %collective-permute-start) | collective-permute-done | bytes 2359328 | tf_op jit(solution)/shard_map/ppermute | solution.py:19
  65.2 5.5 collective-permute-done.1
  70.7 3.9 pad_maximum_fusion
  74.6 3.8 slice_bitcast_fusion
  78.4 4.7 gather_fusion.1
  83.0 3.5 fusion.83
  87.6 4.7 gather_fusion
  92.3 3.7 fusion.84
  98.1 3.6 convolution_bitcast_fusion.5
  101.6 5.2 multiply_reduce_fusion.5
  106.9 3.9 convolution_bitcast_fusion.11
  110.8 3.6 multiply_convert_fusion.5
  118.7 3.6 convolution_bitcast_fusion.4
  122.3 5.2 multiply_reduce_fusion.4
  127.5 4.0 convolution_bitcast_fusion.10
  131.5 3.7 multiply_convert_fusion.4
  139.5 3.6 convolution_bitcast_fusion.3
  143.0 5.2 multiply_reduce_fusion.3
  148.3 4.0 convolution_bitcast_fusion.9
  152.2 3.8 multiply_convert_fusion.3
  160.3 3.6 convolution_bitcast_fusion.2
  163.9 5.2 multiply_reduce_fusion.2
  169.2 4.0 convolution_bitcast_fusion.8
  173.1 3.7 multiply_convert_fusion.2
  181.1 3.6 convolution_bitcast_fusion.1
  184.6 5.2 multiply_reduce_fusion.1
  189.9 4.0 convolution_bitcast_fusion.7
  193.9 3.7 multiply_convert_fusion.1
  198.9 3.8 convolution_bitcast_fusion
  202.7 5.0 multiply_reduce_fusion
  207.8 4.0 convolution_bitcast_fusion.6
  211.7 3.7 multiply_convert_fusion
  217.9 3.3 reshape.1253
  228.7 3.2 scatter_fusion
  262.7 3.3 scatter_fusion.1
  269.8 3.3 scatter_fusion.2
  276.9 3.3 scatter_fusion.3
  283.9 3.3 scatter_fusion.4
  290.9 3.6 scatter_fusion.5
  297.1 5.0 slice_bitcast_fusion.9
  302.0 4.3 copy.292
  308.3 4.7 copy.289
  316.8 3.3 scatter_fusion.6
  322.6 4.3 copy.295
  328.9 4.9 copy.298
  335.7 4.7 copy.301
  342.5 4.7 copy.304
  350.9 3.3 scatter_fusion.7
  358.0 3.3 scatter_fusion.8
  365.1 3.3 scatter_fusion.9
  372.2 3.3 scatter_fusion.10
  379.3 3.5 scatter_fusion.11
  394.6 6.7 %collective-permute-start.3 = (f32[2,1,384,1536]{3,2,1,0:T(8,128)}, f32[2,1,384,1536]{3,2,1,0:T(8,128)}, u32[]{:S(2)}, u32[]{:S(2)}) collective-permute-start(f32[2,1,384,1536]{3,2,1,0:T(8,128)} %pad_maximum_fusion.2), channel_id=1, source_target_pairs={{0,4},{4,8},{8,12},{12,16},{16,20},{20,24},{24,28},{28,32},{32,36}... | collective-permute-start | bytes 14155784 | tf_op jit(solution)/shard_map/ppermute | solution.py:28
  404.9 3.3 copy.278
  421.1 74.4 %collective-permute-done.2 = f32[2,1,384,1536]{3,2,1,0:T(8,128)} collective-permute-done((f32[2,1,384,1536]{3,2,1,0:T(8,128)}, f32[2,1,384,1536]{3,2,1,0:T(8,128)}, u32[]{:S(2)}, u32[]{:S(2)}) %collective-permute-start.2) | collective-permute-done | bytes 4718624 | tf_op jit(solution)/shard_map/ppermute | solution.py:28
  495.5 3.7 collective-permute-done.3
  499.1 7.3 %fusion.21 = (f32[1,384,1536]{2,1,0:T(8,128)S(1)}, bf16[1,1,384,1536]{3,2,1,0:T(8,128)(2,1)}) fusion(f32[2,1,384,1536]{3,2,1,0:T(8,128)} %collective-permute-done.3, f32[2,1,384,1536]{3,2,1,0:T(8,128)} %collective-permute-done.2, f32[3,384,1536]{2,1,0:T(8,128)} %slice_dynamic-update-slice_fusion.6, f32[3,384,1536]{2,1,0:T(8,128)} %slice_dynamic-update-slice_fusion), kind=kLoop, calls=%fused_computation.80 | loop fusion | flops 2949120 | bytes 17694720 | tf_op jit(solution)/shard_map/add | solution.py:153
  508.4 4.9 multiply_reduce_fusion.8
  522.7 4.5 fusion.65
  549.3 3.6 multiply_reduce_fusion.6
  552.9 59.3 %psum.14 = f32[2,128]{1,0:T(2,128)S(1)} all-reduce(f32[2,128]{1,0:T(2,128)S(1)} %pad_maximum_fusion.5), channel_id=1, replica_groups=mesh['pipe'=2,'seq'=16,'dp'=4] {'dp'}, use_global_device_ids=true, to_apply=%region_31.32 | all-reduce | flops 256 | bytes 2048 | tf_op jit(solution)/shard_map/psum | solution.py:161
  612.2 42.3 %psum.15 = f32[2,128]{1,0:T(2,128)S(1)} all-reduce(f32[2,128]{1,0:T(2,128)S(1)} %psum.14), channel_id=1, replica_groups=mesh['pipe'=2,'seq'=16,'dp'=4] {'seq'}, use_global_device_ids=true, to_apply=%region_32.33 | all-reduce | flops 256 | bytes 2048 | tf_op jit(solution)/shard_map/psum | solution.py:161
  655.1 4.0 copy.394
  (274 shorter events, 209.7 us)
Async XLA Ops:
  2.2 2.6 copy-start.2
  4.8 2.2 copy-start.72
  4.8 2.7 copy-start.5
  7.0 15.9 %copy-start.70 = (f32[128]{0:T(128)}, f32[128]{0:T(128)S(1)}, u32[]{:S(2)}) copy-start(f32[128]{0:T(128)S(1)} %get-tuple-element.45) | copy-start | bytes 1540
  8.1 2.3 copy-start.23
  8.8 8.3 %copy-start.55 = (bf16[1,1,1,384,1536]{4,3,2,1,0:T(8,128)(2,1)S(1)}, bf16[1,1,1,384,1536]{4,3,2,1,0:T(8,128)(2,1)}, u32[]{:S(2)}) copy-start(bf16[1,1,1,384,1536]{4,3,2,1,0:T(8,128)(2,1)} %param.9) | copy-start | bytes 3538948
  10.4 8.1 %copy-start.7 = (bf16[1,1,1,384,1536]{4,3,2,1,0:T(8,128)(2,1)S(1)}, bf16[1,1,1,384,1536]{4,3,2,1,0:T(8,128)(2,1)}, u32[]{:S(2)}) copy-start(bf16[1,1,1,384,1536]{4,3,2,1,0:T(8,128)(2,1)} %param.6) | copy-start | bytes 3538948
  10.4 54.8 %collective-permute-start = (bf16[2,1,384,1536]{3,2,1,0:T(8,128)(2,1)}, bf16[2,1,384,1536]{3,2,1,0:T(8,128)(2,1)}, u32[]{:S(2)}, u32[]{:S(2)}) collective-permute-start(bf16[2,1,384,1536]{3,2,1,0:T(8,128)(2,1)} %pad_maximum_fusion.4), channel_id=1, source_target_pairs={{0,4},{4,8},{8,12},{12,16},{16,20},{20,24},{24,28},{28,32},{32,36}... | collective-permute-start | bytes 7077896 | tf_op jit(solution)/shard_map/ppermute | solution.py:19
  15.8 54.9 %collective-permute-start.1 = (bf16[2,1,384,1536]{3,2,1,0:T(8,128)(2,1)}, bf16[2,1,384,1536]{3,2,1,0:T(8,128)(2,1)}, u32[]{:S(2)}, u32[]{:S(2)}) collective-permute-start(bf16[2,1,384,1536]{3,2,1,0:T(8,128)(2,1)} %pad_maximum_fusion.4), channel_id=1, source_target_pairs={{4,0},{8,4},{12,8},{16,12},{20,16},{24,20},{28,24},{32,28},{36,32}... | collective-permute-start | bytes 7077896 | tf_op jit(solution)/shard_map/ppermute | solution.py:20
  20.7 380.6 %copy-start = (f32[384,12,128]{0,2,1:T(8,128)}, f32[384,12,128]{0,2,1:T(8,128)S(1)}, u32[]{:S(2)}) copy-start(f32[384,12,128]{0,2,1:T(8,128)S(1)} %mul.607) | copy-start | bytes 7077892
  22.9 2.0 copy-start.66
  24.9 2.9 copy-start.73
  26.0 44.7 %copy-start.24 = (bf16[1,1,384,1536]{3,2,1,0:T(8,128)(2,1)S(1)}, bf16[1,1,384,1536]{3,2,1,0:T(8,128)(2,1)}, u32[]{:S(2)}) copy-start(bf16[1,1,384,1536]{3,2,1,0:T(8,128)(2,1)} %copy-done.23) | copy-start | bytes 3538948
  36.6 34.1 %copy-start.33 = (bf16[1,1,1,384,1536]{4,3,2,1,0:T(8,128)(2,1)S(1)}, bf16[1,1,1,384,1536]{4,3,2,1,0:T(8,128)(2,1)}, u32[]{:S(2)}) copy-start(bf16[1,1,1,384,1536]{4,3,2,1,0:T(8,128)(2,1)} %param.8) | copy-start | bytes 3538948
  106.9 3.9 copy-start.18
  127.5 4.0 copy-start.19
  148.3 4.0 copy-start.20
  169.2 4.0 copy-start.21
  189.9 4.0 copy-start.22
  198.9 8.9 %copy-start.52 = (bf16[1,1152,256]{1,2,0:T(8,128)(2,1)}, bf16[1,1152,256]{1,2,0:T(8,128)(2,1)S(1)}, u32[]{:S(2)}) copy-start(bf16[1,1152,256]{1,2,0:T(8,128)(2,1)S(1)} %copy.364) | copy-start | bytes 1769476
  198.9 3.8 copy-start.56
  202.7 5.0 copy-start.54
  207.7 4.0 copy-start.17
  211.7 3.7 copy-start.10
  211.7 3.7 copy-start.58
  231.9 2.5 copy-start.12
  231.9 2.5 copy-start.57
  258.3 4.5 copy-start.36
  266.0 3.8 copy-start.42
  273.1 3.8 copy-start.40
  280.1 3.8 copy-start.39
  287.1 3.8 copy-start.38
  297.1 5.0 copy-start.34
  320.0 2.6 copy-start.35
  354.2 3.8 copy-start.45
  361.3 3.8 copy-start.44
  368.4 3.8 copy-start.43
  375.4 3.8 copy-start.37
  385.2 3.1 copy-start.30
  388.3 3.9 copy-start.29
  390.8 104.6 %collective-permute-start.2 = (f32[2,1,384,1536]{3,2,1,0:T(8,128)}, f32[2,1,384,1536]{3,2,1,0:T(8,128)}, u32[]{:S(2)}, u32[]{:S(2)}) collective-permute-start(f32[2,1,384,1536]{3,2,1,0:T(8,128)} %pad_maximum_fusion.1), channel_id=1, source_target_pairs={{4,0},{8,4},{12,8},{16,12},{20,16},{24,20},{28,24},{32,28},{36,32}... | collective-permute-start | bytes 14155784 | tf_op jit(solution)/shard_map/ppermute | solution.py:28
  394.6 104.5 %collective-permute-start.3 = (f32[2,1,384,1536]{3,2,1,0:T(8,128)}, f32[2,1,384,1536]{3,2,1,0:T(8,128)}, u32[]{:S(2)}, u32[]{:S(2)}) collective-permute-start(f32[2,1,384,1536]{3,2,1,0:T(8,128)} %pad_maximum_fusion.2), channel_id=1, source_target_pairs={{0,4},{4,8},{8,12},{12,16},{16,20},{20,24},{24,28},{28,32},{32,36}... | collective-permute-start | bytes 14155784 | tf_op jit(solution)/shard_map/ppermute | solution.py:28
  401.3 2.0 copy-start.62
  404.9 3.3 copy-start.4
  408.2 2.0 copy-start.61
  410.3 2.1 copy-start.47
  410.4 4.3 copy-start.48
  412.4 2.3 copy-start.11
  412.4 3.0 copy-start.13
  412.4 3.0 copy-start.49
  418.8 2.2 copy-start.1
  506.4 2.0 copy-start.69
  506.4 2.0 copy-start.71
  519.5 3.2 copy-start.6
  519.5 3.2 copy-start.65
  522.7 4.6 copy-start.8
  522.7 4.6 copy-start.25
  522.7 4.8 copy-start.26
  522.7 5.5 copy-start.27
  522.7 6.2 copy-start.28
  522.7 6.2 copy-start.67
  532.1 123.0 %collective-permute-start.4 = (bf16[3,1,384,1536]{3,2,1,0:T(8,128)(2,1)}, bf16[3,1,384,1536]{3,2,1,0:T(8,128)(2,1)}, u32[]{:S(2)}, u32[]{:S(2)}) collective-permute-start(bf16[3,1,384,1536]{3,2,1,0:T(8,128)(2,1)} %pad_maximum_fusion.3), channel_id=1, source_target_pairs={{0,64},{64,0},{1,65},{65,1},{2,66},{66,2},{3,67},{67,3},{4,68},{68... | collective-permute-start | bytes 10616840 | tf_op jit(solution)/shard_map/ppermute | solution.py:34
  537.8 3.2 copy-start.59
  541.7 3.2 copy-start.9
  (15 other events, 21.9 us)
